TPU v7x, 128 devices: a whole 4x4x4 slice. The times are simulated.
128 devices in a mesh: rep: 16 (over z_lo, x, core), fsdp: 8 (over z_hi, y).
Axes of the slice: x: 4, y: 4, z: 4 (z_hi: 2, z_lo: 2; z = z_hi * 2 + z_lo), core: 2. Of those that a mesh axis runs over, the one named last changes fastest.
Arguments:
- tokens: bfloat16 [16, 4096, 4096], P('rep', 'fsdp'), may hold values from -6 to 6
- gain: bfloat16 [16, 4096], P('rep', 'fsdp'), may hold values from 0.3984375 to 2
- weight: bfloat16 [16, 4096, 1024], P('rep', 'fsdp'), may hold values from -0.09375 to 0.09375
- w_first: float32 [16, 4096, 1024], P('rep', 'fsdp'), may hold values from -120 to 120
- w_second: float32 [16, 4096, 1024], P('rep', 'fsdp'), may hold values from 10 to 1000
- g_first: float32 [16, 4096], P('rep', 'fsdp'), may hold values from -60 to 60
- g_second: float32 [16, 4096], P('rep', 'fsdp'), may hold values from 10 to 1000
- cotangent: bfloat16 [16, 4096, 1024], P('rep', 'fsdp'), may hold values from -6 to 6
- exponent: int32 [4], replicated, may hold values from 0 to 2
Outputs:
- values: bfloat16 [16, 4096, 1024], P('rep', 'fsdp')
- input_grad: bfloat16 [16, 4096, 4096], P('rep', 'fsdp')
- new_weight: bfloat16 [16, 4096, 1024], P('rep', 'fsdp')
- new_wfirst: float32 [16, 4096, 1024], P('rep', 'fsdp')
- new_wsecond: float32 [16, 4096, 1024], P('rep', 'fsdp')
- new_gain: bfloat16 [16, 4096], P('rep', 'fsdp')
- new_gfirst: float32 [16, 4096], P('rep', 'fsdp')
- new_gsecond: float32 [16, 4096], P('rep', 'fsdp')
Inputs may be any that keep to these rules, and one draw needn't show every extreme that they name: `exponent`: each round's k is the same for all replicas.
All inputs are finite; a program needn't handle non-finite values.
Results may differ from a plain program's by a relative error of at most 0.0068.
Values may be sent and summed in bfloat16 or wider, within the bound.
A program may use at most 128 MiB of HBM per device.

v0:
```python
from functools import partial

import jax
import jax.numpy as jnp
from jax import lax
from jax.sharding import PartitionSpec as P

STEP = 10
ROUNDS = 4


def shortened(shard):

    def short(part):
        return part.astype(jnp.bfloat16) if part.dtype == jnp.float32 else part

    return jax.tree.map(short, shard)


def swapped(value, axis, distance):
    mask = 2**distance
    pairs = [(source, source ^ mask) for source in range(lax.axis_size(axis))]
    return lax.ppermute(value, axis, pairs)


def adam(param, grad, first, second):
    new_first = 0.9 * first + 0.1 * grad
    new_second = 0.95 * second + 0.05 * grad * grad
    fix_first = 1.0 - 0.9**STEP
    fix_second = 1.0 - 0.95**STEP
    pf = param.astype(jnp.float32)
    update = new_first / fix_first / (jnp.sqrt(new_second / fix_second) + 1e-08) + 0.1 * pf
    return ((pf - 0.003 * update).astype(jnp.bfloat16), new_first, new_second)


def pair_with(stepped, bit):
    return jax.tree.map(
        lambda part, own: part.astype(own.dtype), swapped(shortened(stepped), "rep", bit), stepped
    )


def local(tokens, gain, weight, w_first, w_second, g_first, g_second, cotangent, exponent):
    inputs = tokens[0]
    grad_out = cotangent[0]
    rstd = lax.rsqrt(
        jnp.mean(jnp.square(inputs.astype(jnp.float32)), axis=1, keepdims=True) + 1e-05
    )
    w_piece = lax.all_gather(weight[0], "fsdp", axis=0, tiled=True)
    g_piece = lax.all_gather(gain[0], "fsdp", axis=0, tiled=True)
    g_scaled = g_piece.astype(jnp.float32)
    columns = inputs.astype(jnp.float32)
    piece_norm = (columns * rstd * g_scaled[None, :]).astype(jnp.bfloat16)
    acc_values = jnp.dot(piece_norm, w_piece, preferred_element_type=jnp.float32)
    d_piece = lax.dot_general(
        grad_out, w_piece, (((1,), (1,)), ((), ())), preferred_element_type=jnp.float32
    )
    dnorm = d_piece
    gfull = g_scaled
    acc_values, dnorm, normed, gfull = (acc_values, dnorm, piece_norm, gfull)
    values = acc_values.astype(jnp.bfloat16)
    xf = inputs.astype(jnp.float32)
    gain_part = jnp.sum(dnorm * xf * rstd, axis=0)
    scaled = dnorm * gfull[None, :]
    inner = jnp.mean(scaled * xf, axis=1, keepdims=True)
    input_grad = (rstd * (scaled - xf * rstd * rstd * inner)).astype(jnp.bfloat16)
    gain_grad = lax.psum_scatter(gain_part, "fsdp", scatter_dimension=0, tiled=True)
    columns = normed
    weight_grad = lax.psum_scatter(
        lax.dot_general(
            columns, grad_out, (((0,), (0,)), ((), ())), preferred_element_type=jnp.float32
        ),
        "fsdp",
        scatter_dimension=0,
        tiled=True,
    )
    w_step, new_wfirst, new_wsecond = adam(weight[0], weight_grad, w_first[0], w_second[0])
    g_step, new_gfirst, new_gsecond = adam(gain[0], gain_grad, g_first[0], g_second[0])
    bits = lax.axis_size("rep").bit_length() - 1
    branches = [partial(lambda pair, bit: pair_with(pair, bit), bit=level) for level in range(bits)]
    for round_index in range(ROUNDS):
        partner_w, partner_g = lax.switch(exponent[round_index], branches, (w_step, g_step))
        w_step = ((w_step.astype(jnp.float32) + partner_w.astype(jnp.float32)) * 0.5).astype(
            jnp.bfloat16
        )
        g_step = ((g_step.astype(jnp.float32) + partner_g.astype(jnp.float32)) * 0.5).astype(
            jnp.bfloat16
        )
    return (
        values[None],
        input_grad[None],
        w_step[None],
        new_wfirst[None],
        new_wsecond[None],
        g_step[None],
        new_gfirst[None],
        new_gsecond[None],
    )


def solution(mesh):
    in_specs = (
        P("rep", "fsdp", None),
        P("rep", "fsdp"),
        P("rep", "fsdp", None),
        P("rep", "fsdp", None),
        P("rep", "fsdp", None),
        P("rep", "fsdp"),
        P("rep", "fsdp"),
        P("rep", "fsdp", None),
        P(),
    )
    out_specs = (
        P("rep", "fsdp", None),
        P("rep", "fsdp", None),
        P("rep", "fsdp", None),
        P("rep", "fsdp", None),
        P("rep", "fsdp", None),
        P("rep", "fsdp"),
        P("rep", "fsdp"),
        P("rep", "fsdp"),
    )
    return jax.shard_map(local, mesh=mesh, in_specs=in_specs, out_specs=out_specs, check_vma=False)
```

profile of v0, /device:TPU:1, one launch (start us, length us, event | category | flops | bytes accessed | tf_op | source)
XLA Modules:
  0.0 418.8 jit_solution(11389014434873866414)
XLA Ops:
  8.0 28.0 %all-gather = bf16[1,4096]{1,0:T(2,128)(2,1)S(1)} all-gather(bf16[1,512]{1,0:T(2,128)(2,1)} %param.26), channel_id=2, replica_groups=mesh['rep'=16,'fsdp'=8] {'fsdp'}, dimensions={1}, use_global_device_ids=true | all-gather | bytes 9216 | tf_op jit(solution)/shard_map/all_gather | solution.py:49
  36.0 3.1 fusion.11
  39.1 8.3 %fusion.22 = f32[4096,1024]{1,0:T(8,128)} fusion(bf16[1,512,4096]{2,1,0:T(8,128)(2,1)S(1)} %copy-done.1, f32[4096]{0:T(1024)S(1)} %bitcast.96, f32[512]{0:T(512)S(1)} %add_rsqrt_fusion, bf16[1,512,1024]{2,1,0:T(8,128)(2,1)S(1)} %copy-done), kind=kOutput, calls=%fused_computation.24 | convolution fusion | flops 4303355904 | bytes 22038528 | tf_op jit(solution)/shard_map/dot_general | solution.py:69
  52.6 69.6 %all-gather.4.cloned.1.call-done = bf16[1,4096,1024]{2,1,0:T(8,128)(2,1)} async-done(((bf16[1,512,1024]{2,1,0:T(8,128)(2,1)}), bf16[1,4096,1024]{2,1,0:T(8,128)(2,1)}) %all-gather.4.cloned.1.call-update) | async-done | bytes 8388624 | tf_op jit(solution)/shard_map/all_gather | solution.py:48
  122.2 12.3 %fusion.14 = (f32[4096]{0:T(1024)S(1)}, f32[512]{0:T(512)S(1)}, f32[512,4096]{1,0:T(8,128)}) fusion(bf16[1,512,4096]{2,1,0:T(8,128)(2,1)} %param.25, f32[512]{0:T(512)S(1)} %add_rsqrt_fusion, f32[4096]{0:T(1024)S(1)} %bitcast.97, bf16[1,4096,1024]{2,1,0:T(8,128)(2,1)} %all-gather.4.cloned.1.call-done, bf16[1,512,1024]{2,1,0:T(8,128)(2,1)S(1)} %copy-done), kind=kOutput, calls=%fused_computation.16 | convolution fusion | flops 4309642752 | bytes 22056960 | tf_op jit(solution)/shard_map/dot_general | solution.py:54
  134.5 31.1 %all-reduce = f32[4096]{0:T(1024)S(1)} all-reduce(f32[4096]{0:T(1024)S(1)} %get-tuple-element.192), channel_id=5, replica_groups=mesh['rep'=16,'fsdp'=8] {'fsdp'}, use_global_device_ids=true, to_apply=%region_4.0.clone | all-reduce | flops 4096 | bytes 32768
  166.3 7.8 %fusion.24 = bf16[1,512,4096]{2,1,0:T(8,128)(2,1)} fusion(bf16[1,512,4096]{2,1,0:T(8,128)(2,1)} %param.25, f32[512,4096]{1,0:T(8,128)} %get-tuple-element.204, f32[512]{0:T(512)S(1)} %broadcast_multiply_fusion.2, f32[4096]{0:T(1024)S(1)} %bitcast.98, f32[512]{0:T(512)S(1)} %add_rsqrt_fusion), kind=kLoop, calls=%fused_computation.25 | loop fusion | flops 16777216 | bytes 16797696 | tf_op jit(solution)/shard_map/broadcast_in_dim | solution.py:90
  174.1 2.9 copy-done.8
  177.0 5.6 %fusion.47 = bf16[1,512,1024]{2,1,0:T(8,128)(2,1)} fusion(bf16[1,4096,1024]{2,1,0:T(8,128)(2,1)S(1)} %copy-done.8, bf16[1,512,4096]{2,1,0:T(8,128)(2,1)S(1)} %copy-done.2, f32[4096]{0:T(1024)S(1)} %bitcast.99, f32[512]{0:T(512)S(1)} %add_rsqrt_fusion), kind=kOutput, calls=%fused_computation.51 | convolution fusion | flops 4303880192 | bytes 13649920 | tf_op jit(solution)/shard_map/dot_general | solution.py:53
  182.6 132.7 %reduce-scatter.2.cloned.1.call-done = f32[512,1024]{1,0:T(8,128)} async-done(((f32[4096,1024]{1,0:T(8,128)}), f32[512,1024]{1,0:T(8,128)}) %reduce-scatter.2.cloned.1.call-update) | async-done | bytes 2097168 | tf_op jit(solution)/shard_map/reduce_scatter | solution.py:68
  315.2 6.6 %fusion.56 = (f32[1,512,1024]{2,1,0:T(8,128)}, bf16[512,1024]{1,0:T(8,128)(2,1)S(1)}, f32[1,512,1024]{2,1,0:T(8,128)}) fusion(f32[512,1024]{1,0:T(8,128)} %reduce-scatter.2.cloned.1.call-done, f32[1,512,1024]{2,1,0:T(8,128)} %param.29, f32[1,512,1024]{2,1,0:T(8,128)} %param.28, bf16[1,512,1024]{2,1,0:T(8,128)(2,1)S(1)} %copy-done.3), kind=kLoop, calls=%fused_computation.56 | loop fusion | flops 8912896 | bytes 12582912 | tf_op jit(solution)/shard_map/broadcast_in_dim | solution.py:93
  321.9 5.4 %conditional.16 = (bf16[512,1024]{1,0:T(8,128)(2,1)}, bf16[512]{0:T(512)(128)(2,1)}) conditional(s32[]{:T(128)} %bitcast.11, (bf16[512,1024]{1,0:T(8,128)(2,1)S(1)}, bf16[512]{0:T(512)(128)(2,1)S(1)}) %tuple.176, (bf16[512,1024]{1,0:T(8,128)(2,1)S(1)}, bf16[512]{0:T(512)(128)(2,1)S(1)}) %tuple.176, ...), branch_computations={%region_5.0_spmd, %region_6.0_spmd, %region_7.0_spmd, %region_8.0_... | conditional | bytes 4198496
  321.9 3.0 collective-permute-start
  324.8 2.4 collective-permute-done.1
  327.9 1.6 fusion.41
  329.6 26.1 %conditional.17 = (bf16[512,1024]{1,0:T(8,128)(2,1)}, bf16[512]{0:T(512)(128)(2,1)}) conditional(s32[]{:T(128)} %bitcast.15, (bf16[512,1024]{1,0:T(8,128)(2,1)S(1)}, bf16[512]{0:T(512)(128)(2,1)S(1)}) %tuple.177, (bf16[512,1024]{1,0:T(8,128)(2,1)S(1)}, bf16[512]{0:T(512)(128)(2,1)S(1)}) %tuple.177, ...), branch_computations={%region_9.0_spmd, %region_10.0_spmd, %region_11.0_spmd, %region_12... | conditional | bytes 4198496
  329.6 2.8 collective-permute-start.12
  332.6 23.0 %collective-permute-done.13 = bf16[512]{0:T(512)(128)(2,1)} collective-permute-done((bf16[512]{0:T(512)(128)(2,1)S(1)}, bf16[512]{0:T(512)(128)(2,1)}, u32[]{:S(2)}, u32[]{:S(2)}) %collective-permute-start.13) | collective-permute-done | bytes 1056 | tf_op jit(solution)/shard_map/cond/branch_2_fun/ppermute | solution.py:23
  358.0 25.1 %conditional.18 = (bf16[512,1024]{1,0:T(8,128)(2,1)}, bf16[512]{0:T(512)(128)(2,1)}) conditional(s32[]{:T(128)} %bitcast.16, (bf16[512,1024]{1,0:T(8,128)(2,1)S(1)}, bf16[512]{0:T(512)(128)(2,1)S(1)}) %tuple.178, (bf16[512,1024]{1,0:T(8,128)(2,1)S(1)}, bf16[512]{0:T(512)(128)(2,1)S(1)}) %tuple.178, ...), branch_computations={%region_13.0_spmd, %region_14.0_spmd, %region_15.0_spmd, %region_1... | conditional | bytes 4198496
  358.0 2.8 collective-permute-start.20
  361.0 22.1 %collective-permute-done.21 = bf16[512]{0:T(512)(128)(2,1)} collective-permute-done((bf16[512]{0:T(512)(128)(2,1)S(1)}, bf16[512]{0:T(512)(128)(2,1)}, u32[]{:S(2)}, u32[]{:S(2)}) %collective-permute-start.21) | collective-permute-done | bytes 1056 | tf_op jit(solution)/shard_map/cond/branch_2_fun/ppermute | solution.py:23
  385.4 22.7 %conditional.19 = (bf16[512,1024]{1,0:T(8,128)(2,1)}, bf16[512]{0:T(512)(128)(2,1)}) conditional(s32[]{:T(128)} %bitcast.17, (bf16[512,1024]{1,0:T(8,128)(2,1)S(1)}, bf16[512]{0:T(512)(128)(2,1)S(1)}) %tuple.179, (bf16[512,1024]{1,0:T(8,128)(2,1)S(1)}, bf16[512]{0:T(512)(128)(2,1)S(1)}) %tuple.179, ...), branch_computations={%region_17.0_spmd, %region_18.0_spmd, %region_19.0_spmd, %region_2... | conditional | bytes 4198496
  387.0 21.1 %collective-permute-done.27 = bf16[512]{0:T(512)(128)(2,1)} collective-permute-done((bf16[512]{0:T(512)(128)(2,1)S(1)}, bf16[512]{0:T(512)(128)(2,1)}, u32[]{:S(2)}, u32[]{:S(2)}) %collective-permute-start.27) | collective-permute-done | bytes 1056 | tf_op jit(solution)/shard_map/cond/branch_1_fun/ppermute | solution.py:23
  408.8 2.6 fusion.52
  (48 shorter events, 12.0 us)
Async XLA Ops:
  7.2 31.9 %copy-start = (bf16[1,512,1024]{2,1,0:T(8,128)(2,1)S(1)}, bf16[1,512,1024]{2,1,0:T(8,128)(2,1)}, u32[]{:S(2)}) copy-start(bf16[1,512,1024]{2,1,0:T(8,128)(2,1)} %param.32) | copy-start | bytes 3145732
  7.2 115.0 %all-gather.4.cloned.1.call-start = ((), (), s32[]{:S(2)}) async-start(), calls=%async_computation.2 | async-start | bytes 9437184 | tf_op jit(solution)/shard_map/all_gather | solution.py:48
  7.9 307.3 %reduce-scatter.2.cloned.1.call-start = ((), (), s32[]{:S(2)}) async-start(), calls=%async_computation.1 | async-start | bytes 18874368 | tf_op jit(solution)/shard_map/reduce_scatter | solution.py:68
  8.0 31.1 %copy-start.1 = (bf16[1,512,4096]{2,1,0:T(8,128)(2,1)S(1)}, bf16[1,512,4096]{2,1,0:T(8,128)(2,1)}, u32[]{:S(2)}) copy-start(bf16[1,512,4096]{2,1,0:T(8,128)(2,1)} %param.25) | copy-start | bytes 12582916
  47.4 0.7 copy-start.4
  47.4 0.7 copy-start.5
  47.4 3.9 copy-start.9
  47.4 5.1 %copy-start.6 = (f32[1,512]{1,0:T(1,128)S(1)}, f32[1,512]{1,0:T(1,128)}, u32[]{:S(2)}) copy-start(f32[1,512]{1,0:T(1,128)} %param.30) | copy-start | bytes 6148
  47.4 5.2 %copy-start.7 = (f32[1,512]{1,0:T(1,128)S(1)}, f32[1,512]{1,0:T(1,128)}, u32[]{:S(2)}) copy-start(f32[1,512]{1,0:T(1,128)} %param.31) | copy-start | bytes 6148
  166.3 7.8 %copy-start.2 = (bf16[1,512,4096]{2,1,0:T(8,128)(2,1)S(1)}, bf16[1,512,4096]{2,1,0:T(8,128)(2,1)}, u32[]{:S(2)}) copy-start(bf16[1,512,4096]{2,1,0:T(8,128)(2,1)} %param.25) | copy-start | bytes 12582916
  166.3 10.7 %copy-start.8 = (bf16[1,4096,1024]{2,1,0:T(8,128)(2,1)S(1)}, bf16[1,4096,1024]{2,1,0:T(8,128)(2,1)}, u32[]{:S(2)}) copy-start(bf16[1,4096,1024]{2,1,0:T(8,128)(2,1)} %all-gather.4.cloned.1.call-done) | copy-start | bytes 25165828
  177.0 138.2 %copy-start.3 = (bf16[1,512,1024]{2,1,0:T(8,128)(2,1)S(1)}, bf16[1,512,1024]{2,1,0:T(8,128)(2,1)}, u32[]{:S(2)}) copy-start(bf16[1,512,1024]{2,1,0:T(8,128)(2,1)} %param.27) | copy-start | bytes 3145732
  321.9 5.4 %collective-permute-start = (bf16[512,1024]{1,0:T(8,128)(2,1)S(1)}, bf16[512,1024]{1,0:T(8,128)(2,1)}, u32[]{:S(2)}, u32[]{:S(2)}) collective-permute-start(bf16[512,1024]{1,0:T(8,128)(2,1)S(1)} %get-tuple-element.112), channel_id=1, source_target_pairs={{0,8},{8,0},{16,24},{24,16},{32,40},{40,32},{48,56},{56,48},{64,72... | collective-permute-start | bytes 3145736 | tf_op jit(solution)/shard_map/cond/branch_0_fun/ppermute | solution.py:23
  324.8 2.4 collective-permute-start.1
  329.6 26.1 %collective-permute-start.12 = (bf16[512,1024]{1,0:T(8,128)(2,1)S(1)}, bf16[512,1024]{1,0:T(8,128)(2,1)}, u32[]{:S(2)}, u32[]{:S(2)}) collective-permute-start(bf16[512,1024]{1,0:T(8,128)(2,1)S(1)} %get-tuple-element.124), channel_id=1, source_target_pairs={{0,32},{8,40},{16,48},{24,56},{32,0},{40,8},{48,16},{56,24},{64,96... | collective-permute-start | bytes 3145736 | tf_op jit(solution)/shard_map/cond/branch_2_fun/ppermute | solution.py:23
  332.3 23.3 %collective-permute-start.13 = (bf16[512]{0:T(512)(128)(2,1)S(1)}, bf16[512]{0:T(512)(128)(2,1)}, u32[]{:S(2)}, u32[]{:S(2)}) collective-permute-start(bf16[512]{0:T(512)(128)(2,1)S(1)} %get-tuple-element.125), channel_id=1, source_target_pairs={{0,32},{8,40},{16,48},{24,56},{32,0},{40,8},{48,16},{56,24},{64,96... | collective-permute-start | bytes 3080 | tf_op jit(solution)/shard_map/cond/branch_2_fun/ppermute | solution.py:23
  358.0 25.1 %collective-permute-start.20 = (bf16[512,1024]{1,0:T(8,128)(2,1)S(1)}, bf16[512,1024]{1,0:T(8,128)(2,1)}, u32[]{:S(2)}, u32[]{:S(2)}) collective-permute-start(bf16[512,1024]{1,0:T(8,128)(2,1)S(1)} %get-tuple-element.132), channel_id=1, source_target_pairs={{0,32},{8,40},{16,48},{24,56},{32,0},{40,8},{48,16},{56,24},{64,96... | collective-permute-start | bytes 3145736 | tf_op jit(solution)/shard_map/cond/branch_2_fun/ppermute | solution.py:23
  360.7 22.4 %collective-permute-start.21 = (bf16[512]{0:T(512)(128)(2,1)S(1)}, bf16[512]{0:T(512)(128)(2,1)}, u32[]{:S(2)}, u32[]{:S(2)}) collective-permute-start(bf16[512]{0:T(512)(128)(2,1)S(1)} %get-tuple-element.133), channel_id=1, source_target_pairs={{0,32},{8,40},{16,48},{24,56},{32,0},{40,8},{48,16},{56,24},{64,96... | collective-permute-start | bytes 3080 | tf_op jit(solution)/shard_map/cond/branch_2_fun/ppermute | solution.py:23
  385.4 22.6 %collective-permute-start.26 = (bf16[512,1024]{1,0:T(8,128)(2,1)S(1)}, bf16[512,1024]{1,0:T(8,128)(2,1)}, u32[]{:S(2)}, u32[]{:S(2)}) collective-permute-start(bf16[512,1024]{1,0:T(8,128)(2,1)S(1)} %get-tuple-element.138), channel_id=1, source_target_pairs={{0,16},{8,24},{16,0},{24,8},{32,48},{40,56},{48,32},{56,40},{64,80... | collective-permute-start | bytes 3145736 | tf_op jit(solution)/shard_map/cond/branch_1_fun/ppermute | solution.py:23
  386.7 21.4 %collective-permute-start.27 = (bf16[512]{0:T(512)(128)(2,1)S(1)}, bf16[512]{0:T(512)(128)(2,1)}, u32[]{:S(2)}, u32[]{:S(2)}) collective-permute-start(bf16[512]{0:T(512)(128)(2,1)S(1)} %get-tuple-element.139), channel_id=1, source_target_pairs={{0,16},{8,24},{16,0},{24,8},{32,48},{40,56},{48,32},{56,40},{64,80... | collective-permute-start | bytes 3080 | tf_op jit(solution)/shard_map/cond/branch_1_fun/ppermute | solution.py:23
Sparse Core Ops, SparseCore 0:
  10.4 111.8 all-gather.3
  126.2 189.0 reduce-scatter.1
where the time goes:
time: 421 us; the launch traced here: 419 us
  waiting for transfers between devices  272 us (65%)
  blocking collectives  59.1 us (14%)
  other arithmetic  28.3 us (7%)
  matrix products  26.1 us (6%)
  between operations  17.4 us (4%)
  starting transfers between devices  10.7 us (3%)
  local copies, waits for them, and re-layouts  5.37 us (1%)
    reduce_scatter x1, waiting for transfers between devices, local(): lax.psum_scatter(lax.dot_general(columns, grad_out, (((0,), (0,)), ((), (...  133 us
    all_gather x1, waiting for transfers between devices, local(): w_piece = lax.all_gather(weight[0], 'fsdp', axis=0, tiled=True)  69.6 us
    ppermute x8, waiting for transfers between devices, swapped(): return lax.ppermute(value, axis, pairs)  68.6 us
    unnamed x1, blocking collectives  31.1 us
    all_gather x1, blocking collectives, local(): g_piece = lax.all_gather(gain[0], 'fsdp', axis=0, tiled=True)  28 us
    dot_general x1, matrix products, local(): lax.dot_general(grad_out, w_piece, (((1,), (1,)), ((), ())), preferred_el...  12.3 us
    ppermute x8, starting transfers between devices, swapped(): return lax.ppermute(value, axis, pairs)  10.6 us
  transfers between devices with their start and end apart: 10, of which 6 were waited for; matrix products, arithmetic and copies ran while one was open for 9% of the time, Pallas kernels for 0%

commit v1 on v0

v1 whole, which is shorter than its diff:
```python
import functools

import jax
import jax.numpy as jnp
from jax import lax
from jax.experimental import pallas as pl
from jax.experimental.pallas import tpu as pltpu
from jax.sharding import PartitionSpec as P

STEP = 10
ROUNDS = 4
T = 512
B = 512
D = 4096
KV = 1024
NS = 160
NL = 48
GP = 128
MESH = pl.DeviceIdType.MESH
F32 = jnp.float32
BF16 = jnp.bfloat16


def adam(param, grad, first, second):
    new_first = 0.9 * first + 0.1 * grad
    new_second = 0.95 * second + 0.05 * grad * grad
    fix_first = 1.0 - 0.9**STEP
    fix_second = 1.0 - 0.95**STEP
    update = new_first / fix_first / (jnp.sqrt(new_second / fix_second) + 1e-08) + 0.1 * param
    return (param - 0.003 * update).astype(BF16), new_first, new_second


def averaged(parts, exponents):
    for e in exponents:
        mixed = []
        for j in range(8):
            partner = jnp.where(e == 0, parts[j ^ 1], jnp.where(e == 1, parts[j ^ 2], parts[j ^ 4]))
            mixed.append(((parts[j] + partner) * 0.5).astype(BF16).astype(F32))
        parts = mixed
    return parts


def kernel(
    x_hbm, gain_ref, w_hbm, m_hbm, v_hbm, gm_ref, gv_ref, cot_hbm, exp_ref,
    val_hbm, ig_hbm, nw_hbm, nm_hbm, nv_hbm, ng_ref, ngm_ref, ngv_ref,
    xb, nrm, nt, ntp, wb, cot, cotp, acc, own, vout, rstd, slope,
    gb, ggs, ggr, gxs, gxr,
    sd, sr, sl, dr, dl, rr, rl, m_v, v_v, gs, gr, gt, wn,
    ssem, rsem, lsem,
):
    rep = lax.axis_index("rep")
    f = lax.axis_index("fsdp")
    h, y = f // 4, f % 4
    zlo, rank = rep // 8, rep % 8
    bits = (rank % 2, (rank // 2) % 2, rank // 4)

    def shard(dh, dy):
        return (1 - h if dh else h) * 4 + (y + dy) % 4

    def peer(dh, dy):
        return (rep, shard(dh, dy))

    def mate_rank(j):
        return sum((1 - b if (j >> i) & 1 else b) * (1 << i) for i, b in enumerate(bits))

    def mate(j):
        return (zlo * 8 + mate_rank(j), f)

    right, left, across = peer(0, 1), peer(0, 3), peer(1, 0)

    sent, kept = [], []

    def send(src, dst, device):
        i = len(sent)
        copy = pltpu.make_async_remote_copy(
            src_ref=src, dst_ref=dst, send_sem=ssem.at[i], recv_sem=rsem.at[i],
            device_id=device, device_id_type=MESH,
        )
        copy.start()
        sent.append(copy)
        return copy

    def move(src, dst):
        copy = pltpu.make_async_copy(src, dst, lsem.at[len(kept)])
        copy.start()
        kept.append(copy)
        return copy

    def rows(start, size):
        return pl.ds(start, size)

    barrier = pltpu.get_barrier_semaphore()
    others = [peer(i // 4, i % 4) for i in range(1, 8)] + [mate(j) for j in range(1, 8)]
    for device in others:
        pl.semaphore_signal(barrier, inc=1, device_id=device, device_id_type=MESH)
    pl.semaphore_wait(barrier, len(others))

    def send_wz(k):
        return send(w_hbm.at[0, rows(128 * k, 128)], wb.at[4, rows(128 * k, 128)], across)

    wz = [send_wz(0), send_wz(1)]
    a1r = [send(w_hbm.at[0, rows(0, 256)], wb.at[3, rows(0, 256)], right)]
    a1l = [send(w_hbm.at[0, rows(256, 256)], wb.at[1, rows(256, 256)], left)]
    a1r.append(send(w_hbm.at[0, rows(256, 256)], wb.at[3, rows(256, 256)], right))
    a1l.append(send(w_hbm.at[0, rows(0, 256)], wb.at[1, rows(0, 256)], left))

    gb[0] = jnp.broadcast_to(gain_ref[...].astype(F32), (8, B))
    gains = [
        send(gb.at[0], gb.at[4 * (i // 4) + (4 - i % 4) % 4], peer(i // 4, i % 4))
        for i in range(1, 8)
    ]

    def columns(b):
        return pl.ds(pl.multiple_of(shard(b // 4, b % 4) * B, B), B)

    x_in = [move(x_hbm.at[0, :, columns(b)], xb.at[b]) for b in range(8)]
    cot_in = move(cot_hbm.at[0], cot)
    w_in = move(w_hbm.at[0], wb.at[0])
    m_in = move(m_hbm.at[0], m_v)
    v_in = move(v_hbm.at[0], v_v)
    for copy in x_in:
        copy.wait()

    @pl.loop(0, T // 64)
    def _(i):
        r = pl.ds(pl.multiple_of(i * 64, 64), 64)
        total = jnp.zeros((64, B), F32)
        for b in range(8):
            xf = xb[b, r, :].astype(F32)
            total += xf * xf
        mean = jnp.sum(total, axis=1, keepdims=True) * (1.0 / D)
        rstd[r, :] = jnp.broadcast_to(lax.rsqrt(mean + 1e-05), (64, 128))

    for copy in gains:
        copy.wait_recv()

    def normalise(first, last):
        @pl.loop(first, last)
        def _(b):
            g = gb[b, 0:1, :]

            @pl.loop(0, T // 128)
            def _(i):
                r = pl.ds(pl.multiple_of(i * 128, 128), 128)
                tile = (xb[b, r, :].astype(F32) * rstd[r, 0:1] * g).astype(BF16)
                nrm[b, r, :] = tile
                nt[b, :, r] = tile.T

    def forward_wz(k):
        wz[k].wait_recv()
        piece = rows(128 * k, 128)
        return (
            send(wb.at[4, piece], wb.at[7, piece], right),
            send(wb.at[4, piece], wb.at[5, piece], left),
        )

    def add_values(b, first=False):
        @pl.loop(0, KV // 256)
        def _(n):
            c = pl.ds(pl.multiple_of(n * 256, 256), 256)
            part = jnp.dot(nrm[b], wb[b, :, c], preferred_element_type=F32)
            acc[:, c] = part if first else acc[:, c] + part

    a2 = [forward_wz(0)]
    wz.append(send_wz(2))
    normalise(4, 8)
    a2.append(forward_wz(1))
    wz.append(send_wz(3))
    normalise(0, 4)
    w_in.wait()
    add_values(0, True)
    a2.append(forward_wz(2))
    cot_in.wait()
    cot_z = send(cot, cotp, across)
    a2.append(forward_wz(3))

    def send_nt(dy, pair):
        r = rows(256 * pair, 256)
        return send(nt.at[4 + dy, r], ntp.at[dy, r], across)

    nt2 = [send_nt(2, 0), send_nt(2, 1)]

    a1r[0].wait_recv()
    a3r = send(wb.at[3, rows(0, 256)], wb.at[2, rows(0, 256)], right)
    a1l[0].wait_recv()
    a3l = send(wb.at[1, rows(256, 256)], wb.at[2, rows(256, 256)], left)
    a1r[1].wait_recv()
    a1l[1].wait_recv()
    add_values(1)
    add_values(3)
    add_values(4)
    for pair in a2:
        pair[0].wait_recv()
        pair[1].wait_recv()
    a4r = send(wb.at[7, rows(0, 192)], wb.at[6, rows(0, 192)], right)
    a4l = send(wb.at[5, rows(320, 192)], wb.at[6, rows(320, 192)], left)
    add_values(5)
    add_values(7)
    cot_z.wait_recv()
    nt1, nt3, nt0 = [send_nt(1, 0)], [send_nt(3, 0)], []
    a3r.wait_recv()
    a3l.wait_recv()
    a4z = send(wb.at[2, rows(192, 128)], wb.at[6, rows(192, 128)], across)

    def gradient(dy, pair, write):
        r = rows(256 * pair, 256)

        @pl.loop(0, KV // 256)
        def _(n):
            c = pl.ds(pl.multiple_of(n * 256, 256), 256)
            part = jnp.dot(nt[dy, r, :], cot[:, c], preferred_element_type=F32)
            part += jnp.dot(ntp[dy, r, :], cotp[:, c], preferred_element_type=F32)
            write(c, part)

    d2 = []
    for pair in range(2):
        nt2[pair].wait_recv()

        def write(c, part, pair=pair):
            sd[rows(256 * pair, 256), c] = part.astype(BF16)

        gradient(2, pair, write)
        there = rows(128 * pair, 128)
        d2.append(send(sd.at[rows(256 * pair, 128)], dr.at[there], right))
        d2.append(send(sd.at[rows(256 * pair + 128, 128)], dl.at[there], left))
    add_values(2)

    def pass_on(pair):
        (nt1[pair]).wait_recv()
        d2[2 * pair].wait_recv()
        there = rows(128 * pair, 128)
        top, low = rows(256 * pair, 128), rows(256 * pair + 128, 128)

        def write_right(c, part):
            sr[top, c] = (part[:128] + dr[there, c].astype(F32)).astype(BF16)
            sr[low, c] = part[128:].astype(BF16)

        gradient(1, pair, write_right)
        rights = [send(sr.at[r], rr.at[r], right) for r in (top, low)]
        (nt3[pair]).wait_recv()
        d2[2 * pair + 1].wait_recv()

        def write_left(c, part):
            sl[top, c] = part[:128].astype(BF16)
            sl[low, c] = (part[128:] + dl[there, c].astype(F32)).astype(BF16)

        gradient(3, pair, write_left)
        lefts = [send(sl.at[r], rl.at[r], left) for r in (top, low)]
        return list(zip(rights, lefts, strict=True))

    nt1.append(send_nt(1, 1))
    nt3.append(send_nt(3, 1))
    for copy in (a4r, a4l, a4z):
        copy.wait_recv()
    add_values(6)
    arriving = pass_on(0)
    nt0 += [send_nt(0, 0), send_nt(0, 1)]

    @pl.loop(0, T // 64)
    def _(i):
        r = pl.ds(pl.multiple_of(i * 64, 64), 64)
        total = acc[r, :]
        vout[r, :] = total.astype(BF16)
        inner = jnp.sum(total * cot[r, :].astype(F32), axis=1, keepdims=True) * (1.0 / D)
        slope[r, :] = inner * rstd[r, :]

    move(vout, val_hbm.at[0])

    def backward(first, last):
        @pl.loop(first, last)
        def _(b):
            for n in range(B // 256):
                c = pl.ds(n * 256, 256)
                g = gb[b, 0:1, c]
                dn = lax.dot_general(
                    cot[...], wb[b, c, :], (((1,), (1,)), ((), ())), preferred_element_type=F32
                )
                xf = xb[b, :, c].astype(F32)
                rs = rstd[:, 0:1]
                xb[b, :, c] = (rs * (dn * g - xf * slope[:, 0:1])).astype(BF16)
                share = dn * xf * rs
                ggs[b, :, c] = jnp.sum(share.reshape(T // 8, 8, 256), axis=0)

        for b in range(first, last):
            move(xb.at[b], ig_hbm.at[0, :, columns(b)])

    backward(0, 4)
    arriving += pass_on(1)
    backward(4, 8)
    gg = [
        send(ggs.at[i], ggr.at[4 * (i // 4) + (4 - i % 4) % 4], peer(i // 4, i % 4))
        for i in range(1, 8)
    ]

    exponents = [exp_ref[i] for i in range(ROUNDS)]
    m_in.wait()
    v_in.wait()
    n_pieces = B // GP
    out1, out2 = [], []

    def own_gradient(pair):
        nt0[pair].wait_recv()

        def write(c, part):
            own[rows(256 * pair, 256), c] = part

        gradient(0, pair, write)

    def step(p):
        r = rows(GP * p, GP)
        for copy in arriving[p]:
            copy.wait_recv()
        for e in range(8):
            c = pl.ds(128 * e, 128)
            grad = own[r, c] + rr[r, c].astype(F32) + rl[r, c].astype(F32)
            stepped, m_v[r, c], v_v[r, c] = adam(wb[0, r, c].astype(F32), grad, m_v[r, c], v_v[r, c])
            gs[p, e] = stepped
        out1.append([send(gs.at[p, mate_rank(j)], gr.at[p, j], mate(j)) for j in range(1, 8)])
        move(m_v.at[r], nm_hbm.at[0, r])
        move(v_v.at[r], nv_hbm.at[0, r])

    mine = pl.ds(pl.multiple_of(rank * 128, 128), 128)

    def mix(p):
        r = rows(GP * p, GP)
        for copy in out1[p]:
            copy.wait_recv()

        @pl.loop(0, GP // 32)
        def _(i):
            q = pl.ds(pl.multiple_of(i * 32, 32), 32)
            parts = [gs[p, rank, q, :].astype(F32)]
            parts += [gr[p, j, q, :].astype(F32) for j in range(1, 8)]
            parts = averaged(parts, exponents)
            for j in range(8):
                gt[p, j, q, :] = parts[j].astype(BF16)

        out2.append([send(gt.at[p, j], wn.at[r, mine], mate(j)) for j in range(1, 8)])
        wn[r, mine] = gt[p, 0]

    def finish(p):
        r = rows(GP * p, GP)
        for copy in out2[p]:
            copy.wait_recv()
        move(wn.at[r], nw_hbm.at[0, r])

    own_gradient(0)
    step(0)
    step(1)

    for copy in gg:
        copy.wait_recv()
    total = ggs[0]
    for i in range(1, 8):
        total += ggr[i]
    grad = jnp.sum(total, axis=0, keepdims=True)
    stepped, ngm_ref[...], ngv_ref[...] = adam(
        gain_ref[...].astype(F32), grad, gm_ref[...], gv_ref[...]
    )
    gxs[...] = jnp.broadcast_to(stepped.astype(F32), (8, B))
    gx = [send(gxs, gxr.at[j], mate(j)) for j in range(1, 8)]

    mix(0)
    own_gradient(1)
    step(2)
    mix(1)
    for copy in gx:
        copy.wait_recv()
    parts = averaged([gxs[...]] + [gxr[j] for j in range(1, 8)], exponents)
    ng_ref[...] = parts[0][0:1].astype(BF16)
    finish(0)
    step(3)
    mix(2)
    finish(1)
    mix(3)
    finish(2)
    finish(3)

    for copy in sent:
        copy.wait_send()
    for copy in kept[12:]:
        copy.wait()


def local(*args):
    any_space, vmem = pl.BlockSpec(memory_space=pl.ANY), pl.BlockSpec(memory_space=pltpu.VMEM)
    smem = pl.BlockSpec(memory_space=pltpu.SMEM)
    shapes = [
        ((1, T, KV), BF16), ((1, T, D), BF16), ((1, B, KV), BF16), ((1, B, KV), F32), ((1, B, KV), F32),
        ((1, B), BF16), ((1, B), F32), ((1, B), F32),
    ]
    scratch = [
        ((8, T, B), BF16), ((8, T, B), BF16), ((8, B, T), BF16), ((4, B, T), BF16),
        ((8, B, KV), BF16), ((T, KV), BF16), ((T, KV), BF16),
        ((T, KV), F32), ((B, KV), F32), ((T, KV), BF16), ((T, 128), F32), ((T, 128), F32),
        ((8, 8, B), F32), ((8, 8, B), F32), ((8, 8, B), F32), ((8, B), F32), ((8, 8, B), F32),
        ((B, KV), BF16), ((B, KV), BF16), ((B, KV), BF16), ((B // 2, KV), BF16), ((B // 2, KV), BF16),
        ((B, KV), BF16), ((B, KV), BF16), ((B, KV), F32), ((B, KV), F32),
        ((B // GP, 8, GP, 128), BF16), ((B // GP, 8, GP, 128), BF16), ((B // GP, 8, GP, 128), BF16), ((B, KV), BF16),
    ]
    return pl.pallas_call(
        kernel,
        out_shape=[jax.ShapeDtypeStruct(s, t) for s, t in shapes],
        in_specs=[any_space, vmem, any_space, any_space, any_space, vmem, vmem, any_space, smem],
        out_specs=[any_space] * 5 + [vmem] * 3,
        scratch_shapes=[pltpu.VMEM(s, t) for s, t in scratch]
        + [pltpu.SemaphoreType.DMA((NS,)), pltpu.SemaphoreType.DMA((NS,)), pltpu.SemaphoreType.DMA((NL,))],
        compiler_params=pltpu.CompilerParams(
            collective_id=0, has_side_effects=True, vmem_limit_bytes=60 << 20
        ),
        cost_estimate=pl.CostEstimate(flops=6 * T * D * KV, bytes_accessed=20 << 20, transcendentals=0),
        name="layer_step",
    )(*args)


def solution(mesh):
    split, vector = P("rep", "fsdp", None), P("rep", "fsdp")
    return jax.shard_map(
        local,
        mesh=mesh,
        in_specs=(split, vector, split, split, split, vector, vector, split, P()),
        out_specs=(split, split, split, split, split, vector, vector, vector),
        check_vma=False,
    )
```

time: 421 us -> 168 us (0.40)
  waiting for transfers between devices: 272 us -> 0 us
  Pallas kernels: 0 us -> 153 us
  blocking collectives: 59.1 us -> 0 us
  other arithmetic: 28.3 us -> 0 us
  matrix products: 26.1 us -> 0 us
  between operations: 17.4 us -> 0.65 us
  starting transfers between devices: 10.7 us -> 0 us
  local copies, waits for them, and re-layouts: 5.37 us -> 14.4 us
    pallas_call x0 -> x1, Pallas kernels: none -> 153 us  [local(): pl.pallas_call(kernel, out_shape=[jax.ShapeDtypeStruct(s, t) for s, t in...]
    reduce_scatter x1 -> x0, waiting for transfers between devices: 133 us -> none  [local(): lax.psum_scatter(lax.dot_general(columns, grad_out, (((0,), (0,)), ((), (...]
    all_gather x1 -> x0, waiting for transfers between devices: 69.6 us -> none  [local(): w_piece = lax.all_gather(weight[0], 'fsdp', axis=0, tiled=True)]
    ppermute x8 -> x0, waiting for transfers between devices: 68.6 us -> none  [swapped(): return lax.ppermute(value, axis, pairs)]
    unnamed x1 -> x0, blocking collectives: 31.1 us -> none
    all_gather x1 -> x0, blocking collectives: 28 us -> none  [local(): g_piece = lax.all_gather(gain[0], 'fsdp', axis=0, tiled=True)]
    dot_general x3 -> x0, matrix products: 26.1 us -> none  [the longest x1 12.3 us: local(): lax.dot_general(grad_out, w_piece, (((1,), (1,)), ((), ())), preferred_el...]
    broadcast_in_dim x3 -> x0, other arithmetic: 17 us -> none  [the longest x1 7.75 us: local(): input_grad[None]]
  transfers between devices with their start and end apart: 10 -> 0, of which waited for: 6 -> 0; matrix products, arithmetic and copies ran while one was open for 9% -> 0% of each run, Pallas kernels for 0% -> 0%
where the time goes in v1:
time: 168 us
  Pallas kernels  153 us (91%)
  local copies, waits for them, and re-layouts  14.4 us (9%)
    pallas_call x1, Pallas kernels, local(): pl.pallas_call(kernel, out_shape=[jax.ShapeDtypeStruct(s, t) for s, t in...  153 us
    unnamed x20, local copies, waits for them, and re-layouts  14.4 us

profile of v1, /device:TPU:1, one launch (start us, length us, event | category | flops | bytes accessed | tf_op | source)
XLA Modules:
  0.0 167.8 jit_solution(8216664841555859400)
XLA Ops:
  0.6 152.7 %layer_step.1 = (bf16[1,512,1024]{2,1,0:T(8,128)(2,1)}, bf16[1,512,4096]{2,1,0:T(8,128)(2,1)}, bf16[1,512,1024]{2,1,0:T(8,128)(2,1)}, f32[1,512,1024]{2,1,0:T(8,...) custom-call(bf16[1,512,4096]{2,1,0:T(8,128)(2,1)} %x_hbm.1, ...), custom_call_target="tpu_custom_call" | custom-call | flops 12884901888 | bytes 20971520 | tf_op jit(solution)/shard_map/layer_step/pallas_call | solution.py:401
  153.3 2.3 %copy.25 = bf16[1,512,1024]{2,1,0:T(8,128)(2,1)} copy(bf16[1,512,1024]{2,1,0:T(8,128)(2,1)} %get-tuple-element.16) | data formatting | bytes 2097152
  155.6 0.0 copy-start.2
  155.6 4.8 %copy.26 = bf16[1,512,4096]{2,1,0:T(8,128)(2,1)} copy(bf16[1,512,4096]{2,1,0:T(8,128)(2,1)} %get-tuple-element.17) | data formatting | bytes 8388608
  160.4 0.0 copy-done.2
  160.4 0.0 copy-start.1
  160.4 1.0 copy.27
  161.4 1.0 copy-done.1
  162.4 0.0 copy-start
  162.4 1.3 copy.28
  163.7 1.0 copy-done
  164.7 0.0 copy-start.5
  164.7 0.0 copy-start.4
  164.7 0.0 copy-start.3
  164.7 1.3 copy.29
  166.0 0.0 copy-done.5
  166.0 0.6 copy.30
  166.6 0.0 copy-done.4
  166.6 0.6 copy.31
  167.2 0.0 copy-done.3
  167.2 0.6 copy.32
Async XLA Ops:
  155.6 4.8 %copy-start.2 = (bf16[1,512,1024]{2,1,0:T(8,128)(2,1)S(1)}, bf16[1,512,1024]{2,1,0:T(8,128)(2,1)}, u32[]{:S(2)}) copy-start(bf16[1,512,1024]{2,1,0:T(8,128)(2,1)} %get-tuple-element.18) | copy-start | bytes 3145732
  160.4 2.0 %copy-start.1 = (f32[1,512,1024]{2,1,0:T(8,128)S(1)}, f32[1,512,1024]{2,1,0:T(8,128)}, u32[]{:S(2)}) copy-start(f32[1,512,1024]{2,1,0:T(8,128)} %get-tuple-element.19) | copy-start | bytes 6291460
  162.4 2.3 %copy-start = (f32[1,512,1024]{2,1,0:T(8,128)S(1)}, f32[1,512,1024]{2,1,0:T(8,128)}, u32[]{:S(2)}) copy-start(f32[1,512,1024]{2,1,0:T(8,128)} %get-tuple-element.20) | copy-start | bytes 6291460
  164.7 1.3 copy-start.5
  164.7 1.9 %copy-start.4 = (f32[1,512]{1,0:T(1,128)S(1)}, f32[1,512]{1,0:T(1,128)}, u32[]{:S(2)}) copy-start(f32[1,512]{1,0:T(1,128)} %get-tuple-element.22) | copy-start | bytes 6148
  164.7 2.5 %copy-start.3 = (f32[1,512]{1,0:T(1,128)S(1)}, f32[1,512]{1,0:T(1,128)}, u32[]{:S(2)}) copy-start(f32[1,512]{1,0:T(1,128)} %get-tuple-element.23) | copy-start | bytes 6148

commit v2 on v1

v2 whole, which is shorter than its diff:
```python
import functools

import jax
import jax.numpy as jnp
from jax import lax
from jax.experimental import pallas as pl
from jax.experimental.pallas import tpu as pltpu
from jax.sharding import PartitionSpec as P

STEP = 10
ROUNDS = 4
T = 512
B = 512
D = 4096
KV = 1024
NS = 160
NL = 48
PIECES = ((0, 128), (128, 128), (256, 128), (384, 64), (448, 64))
MESH = pl.DeviceIdType.MESH
F32 = jnp.float32
BF16 = jnp.bfloat16


def adam(param, grad, first, second):
    new_first = 0.9 * first + 0.1 * grad
    new_second = 0.95 * second + 0.05 * grad * grad
    fix_first = 1.0 - 0.9**STEP
    fix_second = 1.0 - 0.95**STEP
    update = new_first / fix_first / (jnp.sqrt(new_second / fix_second) + 1e-08) + 0.1 * param
    return (param - 0.003 * update).astype(BF16), new_first, new_second


def averaged(parts, exponents):
    for e in exponents:
        mixed = []
        for j in range(8):
            partner = jnp.where(e == 0, parts[j ^ 1], jnp.where(e == 1, parts[j ^ 2], parts[j ^ 4]))
            mixed.append(((parts[j] + partner) * 0.5).astype(BF16).astype(F32))
        parts = mixed
    return parts


def packed(row):
    return jnp.concatenate([row[:, 128 * i : 128 * (i + 1)] for i in range(4)] + [jnp.zeros((4, 128), F32)], axis=0)


def unpacked(tile):
    return jnp.concatenate([tile[i : i + 1] for i in range(4)], axis=1)


def kernel(
    x_hbm, gain_ref, w_hbm, m_hbm, v_hbm, gm_ref, gv_ref, cot_hbm, exp_ref,
    vout, xb, wn, m_v, v_v, gout,
    nrm, nt, ntp, wb, cot, cotp, acc, own, held, rstd, slope,
    gb, ggs, ggr, gxs, gxr,
    sd, sr, sl, dr, dl, rr, rl, gs, gr, gt,
    ssem, rsem, lsem,
):
    rep = lax.axis_index("rep")
    f = lax.axis_index("fsdp")
    h, y = f // 4, f % 4
    zlo, rank = rep // 8, rep % 8
    bits = (rank % 2, (rank // 2) % 2, rank // 4)

    def shard(dh, dy):
        return (1 - h if dh else h) * 4 + (y + dy) % 4

    def peer(dh, dy):
        return (rep, shard(dh, dy))

    def mate_rank(j):
        return sum((1 - b if (j >> i) & 1 else b) * (1 << i) for i, b in enumerate(bits))

    def mate(j):
        return (zlo * 8 + mate_rank(j), f)

    right, left, across = peer(0, 1), peer(0, 3), peer(1, 0)

    sent, kept = [], []

    def send(src, dst, device):
        i = len(sent)
        copy = pltpu.make_async_remote_copy(
            src_ref=src, dst_ref=dst, send_sem=ssem.at[i], recv_sem=rsem.at[i],
            device_id=device, device_id_type=MESH,
        )
        copy.start()
        sent.append(copy)
        return copy

    def move(src, dst):
        copy = pltpu.make_async_copy(src, dst, lsem.at[len(kept)])
        copy.start()
        kept.append(copy)
        return copy

    def rows(start, size):
        return pl.ds(start, size)

    barrier = pltpu.get_barrier_semaphore()
    others = [peer(i // 4, i % 4) for i in range(1, 8)] + [mate(j) for j in range(1, 8)]
    for device in others:
        pl.semaphore_signal(barrier, inc=1, device_id=device, device_id_type=MESH)
    pl.semaphore_wait(barrier, len(others))

    def back(i):
        return 4 * (i // 4) + (4 - i % 4) % 4

    gb[0] = packed(gain_ref[...].astype(F32))
    gains = [send(gb.at[0], gb.at[back(i)], peer(i // 4, i % 4)) for i in range(1, 8)]

    a1r, a1l, wz = [], [], []
    for k in range(2):
        for pieces, slot, half, device in ((a1r, 3, k, right), (a1l, 1, 1 - k, left)):
            r = rows(256 * half, 256)
            pieces.append(send(w_hbm.at[0, r], wb.at[slot, r], device))
        for q in (2 * k, 2 * k + 1):
            r = rows(128 * q, 128)
            wz.append(send(w_hbm.at[0, r], wb.at[4, r], across))
    cot_z = send(cot_hbm.at[0], cotp, across)

    def columns(b):
        return pl.ds(pl.multiple_of(shard(b // 4, b % 4) * B, B), B)

    x_in = [move(x_hbm.at[0, :, columns(b)], xb.at[b]) for b in range(8)]
    cot_in = move(cot_hbm.at[0], cot)
    w_in = move(w_hbm.at[0], wb.at[0])
    m_in = move(m_hbm.at[0], m_v)
    v_in = move(v_hbm.at[0], v_v)
    for copy in x_in:
        copy.wait()

    @pl.loop(0, T // 64)
    def _(i):
        r = pl.ds(pl.multiple_of(i * 64, 64), 64)
        total = jnp.zeros((64, B), F32)
        for b in range(8):
            xf = xb[b, r, :].astype(F32)
            total += xf * xf
        mean = jnp.sum(total, axis=1, keepdims=True) * (1.0 / D)
        rstd[r, :] = jnp.broadcast_to(lax.rsqrt(mean + 1e-05), (64, 128))

    for copy in gains:
        copy.wait_recv()

    def normalise(first, last):
        @pl.loop(first, last)
        def _(b):
            g = unpacked(gb[b])

            @pl.loop(0, T // 128)
            def _(i):
                r = pl.ds(pl.multiple_of(i * 128, 128), 128)
                tile = (xb[b, r, :].astype(F32) * rstd[r, 0:1] * g).astype(BF16)
                nrm[b, r, :] = tile
                nt[b, :, r] = tile.T

    def forward_wz(k):
        wz[k].wait_recv()
        piece = rows(128 * k, 128)
        return (
            send(wb.at[4, piece], wb.at[7, piece], right),
            send(wb.at[4, piece], wb.at[5, piece], left),
        )

    def add_values(b, first=False):
        @pl.loop(0, KV // 256)
        def _(n):
            c = pl.ds(pl.multiple_of(n * 256, 256), 256)
            part = jnp.dot(nrm[b], wb[b, :, c], preferred_element_type=F32)
            acc[:, c] = part if first else acc[:, c] + part

    def send_nt(dy, pair):
        r = rows(256 * pair, 256)
        return send(nt.at[4 + dy, r], ntp.at[dy, r], across)

    a2 = [forward_wz(0)]
    normalise(4, 8)
    a2.append(forward_wz(1))
    nts = {(dy, 0): send_nt(dy, 0) for dy in (2,)}
    for dy, pair in ((2, 1), (1, 0), (3, 0), (0, 0), (1, 1), (3, 1), (0, 1)):
        nts[dy, pair] = send_nt(dy, pair)
    normalise(0, 4)
    w_in.wait()
    a2.append(forward_wz(2))
    add_values(0, True)
    a2.append(forward_wz(3))

    a1r[0].wait_recv()
    a3r = send(wb.at[3, rows(0, 256)], wb.at[2, rows(0, 256)], right)
    a1l[0].wait_recv()
    a3l = send(wb.at[1, rows(256, 256)], wb.at[2, rows(256, 256)], left)
    a1r[1].wait_recv()
    a1l[1].wait_recv()
    add_values(1)
    add_values(3)
    add_values(4)
    for pair in a2:
        pair[0].wait_recv()
        pair[1].wait_recv()
    a4r = send(wb.at[7, rows(0, 256)], wb.at[6, rows(0, 256)], right)
    a4l = send(wb.at[5, rows(256, 256)], wb.at[6, rows(256, 256)], left)
    add_values(5)
    add_values(7)
    cot_in.wait()
    cot_z.wait_recv()

    def gradient(dy, pair, write):
        r = rows(256 * pair, 256)

        @pl.loop(0, KV // 256)
        def _(n):
            c = pl.ds(pl.multiple_of(n * 256, 256), 256)
            part = jnp.dot(nt[dy, r, :], cot[:, c], preferred_element_type=F32)
            part += jnp.dot(ntp[dy, r, :], cotp[:, c], preferred_element_type=F32)
            write(c, part)

    d2 = []
    for pair in range(2):
        nts[2, pair].wait_recv()

        def write(c, part, pair=pair):
            sd[rows(256 * pair, 256), c] = part.astype(BF16)

        gradient(2, pair, write)
        there = rows(128 * pair, 128)
        d2.append(send(sd.at[rows(256 * pair, 128)], dr.at[there], right))
        d2.append(send(sd.at[rows(256 * pair + 128, 128)], dl.at[there], left))
    a3r.wait_recv()
    a3l.wait_recv()
    add_values(2)

    def partials(pair):
        top, low = rows(256 * pair, 128), rows(256 * pair + 128, 128)

        def write_right(c, part):
            held[0, :, c] = part[:128]
            sr[low, c] = part[128:].astype(BF16)

        def write_left(c, part):
            sl[top, c] = part[:128].astype(BF16)
            held[1, :, c] = part[128:]

        nts[1, pair].wait_recv()
        gradient(1, pair, write_right)
        nts[3, pair].wait_recv()
        gradient(3, pair, write_left)

    def pass_on(pair):
        there = rows(128 * pair, 128)
        start = 256 * pair
        inside = [p for p in PIECES if start <= p[0] < start + 256]
        upper = [p for p in inside if p[0] < start + 128]
        lower = [p for p in inside if p[0] >= start + 128]
        lefts = [send(sl.at[rows(*p)], rl.at[rows(*p)], left) for p in upper]
        d2[2 * pair].wait_recv()
        top, low = rows(start, 128), rows(start + 128, 128)
        sr[top, :] = (held[0] + dr[there, :].astype(F32)).astype(BF16)
        rights = [send(sr.at[rows(*p)], rr.at[rows(*p)], right) for p in upper + lower]
        d2[2 * pair + 1].wait_recv()
        sl[low, :] = (held[1] + dl[there, :].astype(F32)).astype(BF16)
        lefts += [send(sl.at[rows(*p)], rl.at[rows(*p)], left) for p in lower]
        return list(zip(rights, lefts, strict=True))

    partials(0)
    for copy in (a4r, a4l):
        copy.wait_recv()
    add_values(6)
    arriving = pass_on(0)

    @pl.loop(0, T // 64)
    def _(i):
        r = pl.ds(pl.multiple_of(i * 64, 64), 64)
        total = acc[r, :]
        vout[r, :] = total.astype(BF16)
        inner = jnp.sum(total * cot[r, :].astype(F32), axis=1, keepdims=True) * (1.0 / D)
        slope[r, :] = inner * rstd[r, :]

    def backward(first, last):
        @pl.loop(first, last)
        def _(b):
            for n in range(B // 256):
                c = pl.ds(n * 256, 256)
                g = unpacked(gb[b])[:, n * 256 : (n + 1) * 256]
                dn = lax.dot_general(
                    cot[...], wb[b, c, :], (((1,), (1,)), ((), ())), preferred_element_type=F32
                )
                xf = xb[b, :, c].astype(F32)
                rs = rstd[:, 0:1]
                xb[b, :, c] = (rs * (dn * g - xf * slope[:, 0:1])).astype(BF16)
                share = jnp.sum(dn * xf * rs, axis=0, keepdims=True)
                for i in range(2):
                    ggs[b, 2 * n + i : 2 * n + i + 1, :] = share[:, 128 * i : 128 * (i + 1)]

    ggs[...] = jnp.zeros_like(ggs)
    backward(0, 8)
    gg = [send(ggs.at[i], ggr.at[back(i)], peer(i // 4, i % 4)) for i in range(1, 8)]

    exponents = [exp_ref[i] for i in range(ROUNDS)]
    m_in.wait()
    v_in.wait()
    out1, out2 = [], []

    def own_gradient(pair):
        nts[0, pair].wait_recv()

        def write(c, part):
            own[rows(256 * pair, 256), c] = part

        gradient(0, pair, write)

    def step(p):
        r = rows(*PIECES[p])
        for copy in arriving[p]:
            copy.wait_recv()
        for e in range(8):
            c = pl.ds(128 * e, 128)
            grad = own[r, c] + rr[r, c].astype(F32) + rl[r, c].astype(F32)
            stepped, m_v[r, c], v_v[r, c] = adam(wb[0, r, c].astype(F32), grad, m_v[r, c], v_v[r, c])
            gs[e, r, :] = stepped
        out1.append([send(gs.at[mate_rank(j), r], gr.at[j, r], mate(j)) for j in range(1, 8)])

    mine = pl.ds(pl.multiple_of(rank * 128, 128), 128)

    def mix(p):
        r = rows(*PIECES[p])
        for copy in out1[p]:
            copy.wait_recv()

        start, size = PIECES[p]

        @pl.loop(0, size // 32)
        def _(i):
            q = pl.ds(pl.multiple_of(start + i * 32, 32), 32)
            parts = [gs[rank, q, :].astype(F32)] + [gr[j, q, :].astype(F32) for j in range(1, 8)]
            parts = averaged(parts, exponents)
            for j in range(8):
                gt[j, q, :] = parts[j].astype(BF16)

        out2.append([send(gt.at[j, r], wn.at[r, mine], mate(j)) for j in range(1, 8)])
        wn[r, mine] = gt[0, r, :]

    own_gradient(0)
    partials(1)
    arriving += pass_on(1)
    step(0)
    step(1)
    own_gradient(1)
    mix(0)

    for copy in gg:
        copy.wait_recv()
    total = ggs[0]
    for i in range(1, 8):
        total += ggr[i]
    stepped, first, second = adam(gain_ref[...].astype(F32), unpacked(total), gm_ref[...], gv_ref[...])
    gout[1:2, :] = first
    gout[2:3, :] = second
    gxs[...] = packed(stepped.astype(F32))
    gx = [send(gxs, gxr.at[j], mate(j)) for j in range(1, 8)]

    mix(1)
    step(2)
    for copy in gx:
        copy.wait_recv()
    parts = averaged([gxs[...]] + [gxr[j] for j in range(1, 8)], exponents)
    gout[0:1, :] = unpacked(parts[0])
    mix(2)
    step(3)
    step(4)
    mix(3)
    mix(4)
    for copies in out2:
        for copy in copies:
            copy.wait_recv()

    for copy in sent:
        copy.wait_send()


def write_out(vout, xb, wn, m_v, v_v, gout, val, ig, nw, nm, nv, ng, ngm, ngv, sem):
    f = lax.axis_index("fsdp")
    h, y = f // 4, f % 4
    pairs = [(vout, val.at[0]), (wn, nw.at[0]), (m_v, nm.at[0]), (v_v, nv.at[0])]
    for b in range(8):
        column = ((1 - h if b // 4 else h) * 4 + (y + b % 4) % 4) * B
        pairs.append((xb.at[b], ig.at[0, :, pl.ds(pl.multiple_of(column, B), B)]))
    copies = [pltpu.make_async_copy(src, dst, sem.at[i]) for i, (src, dst) in enumerate(pairs)]
    for copy in copies:
        copy.start()
    ng[...] = gout[0:1, :].astype(BF16)
    ngm[...] = gout[1:2, :]
    ngv[...] = gout[2:3, :]
    for copy in copies:
        copy.wait()


def local(*args):
    any_space, vmem = pl.BlockSpec(memory_space=pl.ANY), pl.BlockSpec(memory_space=pltpu.VMEM)
    smem = pl.BlockSpec(memory_space=pltpu.SMEM)
    shapes = [
        ((1, T, KV), BF16), ((1, T, D), BF16), ((1, B, KV), BF16), ((1, B, KV), F32), ((1, B, KV), F32),
        ((1, B), BF16), ((1, B), F32), ((1, B), F32),
    ]
    held = [
        ((T, KV), BF16), ((8, T, B), BF16), ((B, KV), BF16), ((B, KV), F32), ((B, KV), F32), ((8, B), F32),
    ]
    scratch = [
        ((8, T, B), BF16), ((8, B, T), BF16), ((4, B, T), BF16),
        ((8, B, KV), BF16), ((T, KV), BF16), ((T, KV), BF16),
        ((T, KV), F32), ((B, KV), F32), ((2, 128, KV), F32), ((T, 128), F32), ((T, 128), F32),
        ((8, 8, 128), F32), ((8, 8, 128), F32), ((8, 8, 128), F32), ((8, 128), F32), ((8, 8, 128), F32),
        ((B, KV), BF16), ((B, KV), BF16), ((B, KV), BF16), ((B // 2, KV), BF16), ((B // 2, KV), BF16),
        ((B, KV), BF16), ((B, KV), BF16),
        ((8, B, 128), BF16), ((8, B, 128), BF16), ((8, B, 128), BF16),
    ]
    results = pl.pallas_call(
        kernel,
        out_shape=[pltpu.VMEM(s, t) for s, t in held],
        in_specs=[any_space, vmem, any_space, any_space, any_space, vmem, vmem, any_space, smem],
        out_specs=[vmem] * len(held),
        scratch_shapes=[pltpu.VMEM(s, t) for s, t in scratch]
        + [pltpu.SemaphoreType.DMA((NS,)), pltpu.SemaphoreType.DMA((NS,)), pltpu.SemaphoreType.DMA((NL,))],
        compiler_params=pltpu.CompilerParams(
            collective_id=0, has_side_effects=True, vmem_limit_bytes=46 << 20
        ),
        cost_estimate=pl.CostEstimate(flops=6 * T * D * KV, bytes_accessed=20 << 20, transcendentals=0),
        name="layer_step",
    )(*args)
    return pl.pallas_call(
        write_out,
        out_shape=[jax.ShapeDtypeStruct(s, t) for s, t in shapes],
        in_specs=[vmem] * len(held),
        out_specs=[any_space] * 5 + [vmem] * 3,
        scratch_shapes=[pltpu.SemaphoreType.DMA((12,))],
        compiler_params=pltpu.CompilerParams(vmem_limit_bytes=4 << 20),
        name="write_out",
    )(*[pltpu.with_memory_space_constraint(r, pltpu.VMEM) for r in results])


def solution(mesh):
    split, vector = P("rep", "fsdp", None), P("rep", "fsdp")
    return jax.shard_map(
        local,
        mesh=mesh,
        in_specs=(split, vector, split, split, split, vector, vector, split, P()),
        out_specs=(split, split, split, split, split, vector, vector, vector),
        check_vma=False,
    )
```

time: 168 us -> 140 us (0.83)
  local copies, waits for them, and re-layouts: 14.4 us -> 0 us
  Pallas kernels: 153 us -> 139 us
    unnamed x20 -> x0, local copies, waits for them, and re-layouts: 14.4 us -> none
    pallas_call x1 -> x2, Pallas kernels: 153 us -> 139 us  [the longest x1 134 us: local(): pl.pallas_call(kernel, out_shape=[pltpu.VMEM(s, t) for s, t in held], in_...]
where the time goes in v2:
time: 140 us; the launch traced here: 139 us
  Pallas kernels  139 us (99%)
    pallas_call x1, Pallas kernels, local(): pl.pallas_call(kernel, out_shape=[pltpu.VMEM(s, t) for s, t in held], in_...  134 us
    pallas_call x1, Pallas kernels, local(): pl.pallas_call(write_out, out_shape=[jax.ShapeDtypeStruct(s, t) for s, t...  4.6 us

profile of v2, /device:TPU:1, one launch (start us, length us, event | category | flops | bytes accessed | tf_op | source)
XLA Modules:
  0.0 139.5 jit_solution(3956031721706686895)
XLA Ops:
  0.6 134.2 %layer_step.1 = (bf16[512,1024]{1,0:T(8,128)(2,1)S(1)}, bf16[8,512,512]{2,1,0:T(8,128)(2,1)S(1)}, bf16[512,1024]{1,0:T(8,128)(2,1)S(1)}, f32[512,1024]{1,0:T(8,1...) custom-call(bf16[1,512,4096]{2,1,0:T(8,128)(2,1)} %x_hbm.1, bf16[1,512]{1,0:T(2,128)(2,1)} %gain_ref.1, ...), custom_call_target="tpu_custom_call" | custom-call | flops 12884901888 | bytes 20971520 | tf_op jit(solution)/shard_map/layer_step/pallas_call | solution.py:417
  134.9 4.6 %write_out.1 = (bf16[1,512,1024]{2,1,0:T(8,128)(2,1)}, bf16[1,512,4096]{2,1,0:T(8,128)(2,1)}, bf16[1,512,1024]{2,1,0:T(8,128)(2,1)}, f32[1,512,1024]{2,1,0:T(8,1...) custom-call(bf16[512,1024]{1,0:T(8,128)(2,1)S(1)} %get-tuple-element.14.vout, ...), custom_call_target="tpu_custom_call" | custom-call | tf_op jit(solution)/shard_map/write_out/pallas_call | solution.py:430

commit v3 on v2

--- a/solution.py
+++ b/solution.py
@@ -13,9 +13,9 @@
 B = 512
 D = 4096
 KV = 1024
-NS = 160
+NS = 192
 NL = 48
-PIECES = ((0, 128), (128, 128), (256, 128), (384, 64), (448, 64))
+PIECES = ((0, 128), (128, 128), (256, 64), (320, 64), (384, 64), (448, 64))
 MESH = pl.DeviceIdType.MESH
 F32 = jnp.float32
 BF16 = jnp.bfloat16
@@ -53,7 +53,7 @@
     vout, xb, wn, m_v, v_v, gout,
     nrm, nt, ntp, wb, cot, cotp, acc, own, held, rstd, slope,
     gb, ggs, ggr, gxs, gxr,
-    sd, sr, sl, dr, dl, rr, rl, gs, gr, gt,
+    sd, sr, sl, dr, dl, rr, rl, gs, gr, gt, gf,
     ssem, rsem, lsem,
 ):
     rep = lax.axis_index("rep")
@@ -87,6 +87,13 @@
         copy.start()
         sent.append(copy)
         return copy
+
+    def settle(last):
+        while settled[0] < last:
+            sent[settled[0]].wait_send()
+            settled[0] += 1
+
+    settled = [0]
 
     def move(src, dst):
         copy = pltpu.make_async_copy(src, dst, lsem.at[len(kept)])
@@ -215,58 +222,94 @@
             part += jnp.dot(ntp[dy, r, :], cotp[:, c], preferred_element_type=F32)
             write(c, part)
 
-    d2 = []
-    for pair in range(2):
+    def far_gradient(pair):
         nts[2, pair].wait_recv()
 
-        def write(c, part, pair=pair):
+        def write(c, part):
             sd[rows(256 * pair, 256), c] = part.astype(BF16)
 
         gradient(2, pair, write)
-        there = rows(128 * pair, 128)
-        d2.append(send(sd.at[rows(256 * pair, 128)], dr.at[there], right))
-        d2.append(send(sd.at[rows(256 * pair + 128, 128)], dl.at[there], left))
+
+    d2 = {}
+
+    def send_far(pair):
+        d2[pair] = []
+        for start in (0, 64):
+            there = rows(128 * pair + start, 64)
+            top, low = rows(256 * pair + start, 64), rows(256 * pair + 128 + start, 64)
+            d2[pair].append((send(sd.at[top], dr.at[there], right), send(sd.at[low], dl.at[there], left)))
+
+    far_gradient(0)
+    send_far(0)
+    far_gradient(1)
     a3r.wait_recv()
     a3l.wait_recv()
     add_values(2)
 
-    def partials(pair):
-        top, low = rows(256 * pair, 128), rows(256 * pair + 128, 128)
-
-        def write_right(c, part):
+    def partial_right(pair):
+        def write(c, part):
             held[0, :, c] = part[:128]
-            sr[low, c] = part[128:].astype(BF16)
-
-        def write_left(c, part):
-            sl[top, c] = part[:128].astype(BF16)
+            sr[rows(256 * pair + 128, 128), c] = part[128:].astype(BF16)
+
+        nts[1, pair].wait_recv()
+        gradient(1, pair, write)
+
+    def partial_left(pair):
+        def write(c, part):
+            sl[rows(256 * pair, 128), c] = part[:128].astype(BF16)
             held[1, :, c] = part[128:]
 
-        nts[1, pair].wait_recv()
-        gradient(1, pair, write_right)
         nts[3, pair].wait_recv()
-        gradient(3, pair, write_left)
-
-    def pass_on(pair):
-        there = rows(128 * pair, 128)
+        gradient(3, pair, write)
+
+    arriving = {}
+
+    def to_right(start):
+        r = rows(start, 64)
+        arriving[start].append(send(sr.at[r], rr.at[r], right))
+
+    def to_left(start):
+        r = rows(start, 64)
+        arriving[start].append(send(sl.at[r], rl.at[r], left))
+
+    def sum_right(pair, k):
+        d2[pair][k][0].wait_recv()
+        start = 256 * pair + 64 * k
+        far = dr[rows(128 * pair + 64 * k, 64), :].astype(F32)
+        sr[rows(start, 64), :] = (held[0, rows(64 * k, 64), :] + far).astype(BF16)
+        to_right(start)
+
+    def sum_left(pair, k):
+        d2[pair][k][1].wait_recv()
+        start = 256 * pair + 128 + 64 * k
+        far = dl[rows(128 * pair + 64 * k, 64), :].astype(F32)
+        sl[rows(start, 64), :] = (held[1, rows(64 * k, 64), :] + far).astype(BF16)
+        to_left(start)
+
+    def pass_on(pair, between):
         start = 256 * pair
-        inside = [p for p in PIECES if start <= p[0] < start + 256]
-        upper = [p for p in inside if p[0] < start + 128]
-        lower = [p for p in inside if p[0] >= start + 128]
-        lefts = [send(sl.at[rows(*p)], rl.at[rows(*p)], left) for p in upper]
-        d2[2 * pair].wait_recv()
-        top, low = rows(start, 128), rows(start + 128, 128)
-        sr[top, :] = (held[0] + dr[there, :].astype(F32)).astype(BF16)
-        rights = [send(sr.at[rows(*p)], rr.at[rows(*p)], right) for p in upper + lower]
-        d2[2 * pair + 1].wait_recv()
-        sl[low, :] = (held[1] + dl[there, :].astype(F32)).astype(BF16)
-        lefts += [send(sl.at[rows(*p)], rl.at[rows(*p)], left) for p in lower]
-        return list(zip(rights, lefts, strict=True))
-
-    partials(0)
+        for k in range(4):
+            arriving[start + 64 * k] = []
+        to_left(start)
+        to_left(start + 64)
+        sum_right(pair, 0)
+        sum_left(pair, 0)
+        between()
+        sum_right(pair, 1)
+        to_right(start + 128)
+        to_right(start + 192)
+        sum_left(pair, 1)
+
+    partial_right(0)
+    partial_left(0)
     for copy in (a4r, a4l):
         copy.wait_recv()
-    add_values(6)
-    arriving = pass_on(0)
+
+    def middle():
+        add_values(6)
+
+    pass_on(0, middle)
+    send_far(1)
 
     @pl.loop(0, T // 64)
     def _(i):
@@ -293,8 +336,7 @@
                     ggs[b, 2 * n + i : 2 * n + i + 1, :] = share[:, 128 * i : 128 * (i + 1)]
 
     ggs[...] = jnp.zeros_like(ggs)
-    backward(0, 8)
-    gg = [send(ggs.at[i], ggr.at[back(i)], peer(i // 4, i % 4)) for i in range(1, 8)]
+    backward(0, 4)
 
     exponents = [exp_ref[i] for i in range(ROUNDS)]
     m_in.wait()
@@ -311,16 +353,15 @@
 
     def step(p):
         r = rows(*PIECES[p])
-        for copy in arriving[p]:
-            copy.wait_recv()
+        for start in range(PIECES[p][0], sum(PIECES[p]), 64):
+            for copy in arriving[start]:
+                copy.wait_recv()
         for e in range(8):
             c = pl.ds(128 * e, 128)
             grad = own[r, c] + rr[r, c].astype(F32) + rl[r, c].astype(F32)
             stepped, m_v[r, c], v_v[r, c] = adam(wb[0, r, c].astype(F32), grad, m_v[r, c], v_v[r, c])
             gs[e, r, :] = stepped
         out1.append([send(gs.at[mate_rank(j), r], gr.at[j, r], mate(j)) for j in range(1, 8)])
-
-    mine = pl.ds(pl.multiple_of(rank * 128, 128), 128)
 
     def mix(p):
         r = rows(*PIECES[p])
@@ -337,16 +378,29 @@
             for j in range(8):
                 gt[j, q, :] = parts[j].astype(BF16)
 
-        out2.append([send(gt.at[j, r], wn.at[r, mine], mate(j)) for j in range(1, 8)])
-        wn[r, mine] = gt[0, r, :]
+        out2.append([send(gt.at[j, r], gf.at[rank, r], mate(j)) for j in range(1, 8)])
+        gf[rank, r, :] = gt[0, r, :]
+
+    def finish(p):
+        r = rows(*PIECES[p])
+        for copy in out2[p]:
+            copy.wait_recv()
+        for e in range(8):
+            wn[r, 128 * e : 128 * (e + 1)] = gf[e, r, :]
 
     own_gradient(0)
-    partials(1)
-    arriving += pass_on(1)
     step(0)
+    backward(4, 8)
+    gg = [send(ggs.at[i], ggr.at[back(i)], peer(i // 4, i % 4)) for i in range(1, 8)]
+    partial_right(1)
     step(1)
+    partial_left(1)
+    early = len(sent)
+    pass_on(1, lambda: mix(0))
+    ready = len(sent)
     own_gradient(1)
-    mix(0)
+    mix(1)
+    settle(early)
 
     for copy in gg:
         copy.wait_recv()
@@ -359,23 +413,26 @@
     gxs[...] = packed(stepped.astype(F32))
     gx = [send(gxs, gxr.at[j], mate(j)) for j in range(1, 8)]
 
-    mix(1)
     step(2)
+    finish(0)
+    step(3)
     for copy in gx:
         copy.wait_recv()
     parts = averaged([gxs[...]] + [gxr[j] for j in range(1, 8)], exponents)
     gout[0:1, :] = unpacked(parts[0])
+    finish(1)
+    step(4)
+    step(5)
     mix(2)
-    step(3)
-    step(4)
     mix(3)
+    settle(ready)
     mix(4)
-    for copies in out2:
-        for copy in copies:
-            copy.wait_recv()
-
-    for copy in sent:
-        copy.wait_send()
+    mix(5)
+    settle(len(sent) - 28)
+    for p in range(2, len(PIECES)):
+        finish(p)
+
+    settle(len(sent))
 
 
 def write_out(vout, xb, wn, m_v, v_v, gout, val, ig, nw, nm, nv, ng, ngm, ngv, sem):
@@ -412,7 +469,7 @@
         ((8, 8, 128), F32), ((8, 8, 128), F32), ((8, 8, 128), F32), ((8, 128), F32), ((8, 8, 128), F32),
         ((B, KV), BF16), ((B, KV), BF16), ((B, KV), BF16), ((B // 2, KV), BF16), ((B // 2, KV), BF16),
         ((B, KV), BF16), ((B, KV), BF16),
-        ((8, B, 128), BF16), ((8, B, 128), BF16), ((8, B, 128), BF16),
+        ((8, B, 128), BF16), ((8, B, 128), BF16), ((8, B, 128), BF16), ((8, B, 128), BF16),
     ]
     results = pl.pallas_call(
         kernel,

time: 140 us -> 132 us (0.943)
  Pallas kernels: 139 us -> 131 us
    pallas_call x1, Pallas kernels: 134 us -> 127 us  [local(): pl.pallas_call(kernel, out_shape=[pltpu.VMEM(s, t) for s, t in held], in_...]
where the time goes in v3:
time: 132 us
  Pallas kernels  131 us (99%)
    pallas_call x1, Pallas kernels, local(): pl.pallas_call(kernel, out_shape=[pltpu.VMEM(s, t) for s, t in held], in_...  127 us
    pallas_call x1, Pallas kernels, local(): pl.pallas_call(write_out, out_shape=[jax.ShapeDtypeStruct(s, t) for s, t...  4.6 us

profile of v3, /device:TPU:1, one launch (start us, length us, event | category | flops | bytes accessed | tf_op | source)
XLA Modules:
  0.0 131.8 jit_solution(1782463736429165289)
XLA Ops:
  0.6 126.6 %layer_step.1 = (bf16[512,1024]{1,0:T(8,128)(2,1)S(1)}, bf16[8,512,512]{2,1,0:T(8,128)(2,1)S(1)}, bf16[512,1024]{1,0:T(8,128)(2,1)S(1)}, f32[512,1024]{1,0:T(8,1...) custom-call(bf16[1,512,4096]{2,1,0:T(8,128)(2,1)} %x_hbm.1, bf16[1,512]{1,0:T(2,128)(2,1)} %gain_ref.1, ...), custom_call_target="tpu_custom_call" | custom-call | flops 12884901888 | bytes 20971520 | tf_op jit(solution)/shard_map/layer_step/pallas_call | solution.py:474
  127.2 4.6 %write_out.1 = (bf16[1,512,1024]{2,1,0:T(8,128)(2,1)}, bf16[1,512,4096]{2,1,0:T(8,128)(2,1)}, bf16[1,512,1024]{2,1,0:T(8,128)(2,1)}, f32[1,512,1024]{2,1,0:T(8,1...) custom-call(bf16[512,1024]{1,0:T(8,128)(2,1)S(1)} %get-tuple-element.14.vout, ...), custom_call_target="tpu_custom_call" | custom-call | tf_op jit(solution)/shard_map/write_out/pallas_call | solution.py:487

commit v4 on v3

--- a/solution.py
+++ b/solution.py
@@ -113,9 +113,6 @@
     def back(i):
         return 4 * (i // 4) + (4 - i % 4) % 4
 
-    gb[0] = packed(gain_ref[...].astype(F32))
-    gains = [send(gb.at[0], gb.at[back(i)], peer(i // 4, i % 4)) for i in range(1, 8)]
-
     a1r, a1l, wz = [], [], []
     for k in range(2):
         for pieces, slot, half, device in ((a1r, 3, k, right), (a1l, 1, 1 - k, left)):
@@ -124,6 +121,9 @@
         for q in (2 * k, 2 * k + 1):
             r = rows(128 * q, 128)
             wz.append(send(w_hbm.at[0, r], wb.at[4, r], across))
+        if k == 0:
+            gb[0] = packed(gain_ref[...].astype(F32))
+            gains = [send(gb.at[0], gb.at[back(i)], peer(i // 4, i % 4)) for i in range(1, 8)]
     cot_z = send(cot_hbm.at[0], cotp, across)
 
     def columns(b):
@@ -205,8 +205,8 @@
     for pair in a2:
         pair[0].wait_recv()
         pair[1].wait_recv()
-    a4r = send(wb.at[7, rows(0, 256)], wb.at[6, rows(0, 256)], right)
-    a4l = send(wb.at[5, rows(256, 256)], wb.at[6, rows(256, 256)], left)
+    a4r = send(wb.at[7, rows(0, 192)], wb.at[6, rows(0, 192)], right)
+    a4l = send(wb.at[5, rows(320, 192)], wb.at[6, rows(320, 192)], left)
     add_values(5)
     add_values(7)
     cot_in.wait()
@@ -244,6 +244,7 @@
     far_gradient(1)
     a3r.wait_recv()
     a3l.wait_recv()
+    a4z = send(wb.at[2, rows(192, 128)], wb.at[6, rows(192, 128)], across)
     add_values(2)
 
     def partial_right(pair):
@@ -302,22 +303,32 @@
 
     partial_right(0)
     partial_left(0)
-    for copy in (a4r, a4l):
-        copy.wait_recv()
-
-    def middle():
-        add_values(6)
-
-    pass_on(0, middle)
+    pass_on(0, lambda: None)
     send_far(1)
 
-    @pl.loop(0, T // 64)
-    def _(i):
-        r = pl.ds(pl.multiple_of(i * 64, 64), 64)
-        total = acc[r, :]
-        vout[r, :] = total.astype(BF16)
-        inner = jnp.sum(total * cot[r, :].astype(F32), axis=1, keepdims=True) * (1.0 / D)
-        slope[r, :] = inner * rstd[r, :]
+    def slopes():
+        @pl.loop(0, T // 64)
+        def _(i):
+            r = pl.ds(pl.multiple_of(i * 64, 64), 64)
+            total = acc[r, :]
+            vout[r, :] = total.astype(BF16)
+            inner = jnp.sum(total * cot[r, :].astype(F32), axis=1, keepdims=True) * (1.0 / D)
+            slope[r, :] = inner * rstd[r, :]
+
+    def product(b, n):
+        c = pl.ds(n * 256, 256)
+        return lax.dot_general(
+            cot[...], wb[b, c, :], (((1,), (1,)), ((), ())), preferred_element_type=F32
+        )
+
+    def gain_shares(first, last):
+        @pl.loop(first, last)
+        def _(b):
+            for n in range(B // 256):
+                xf = xb[b, :, n * 256 : (n + 1) * 256].astype(F32)
+                share = jnp.sum(product(b, n) * xf * rstd[:, 0:1], axis=0, keepdims=True)
+                for i in range(2):
+                    ggs[b, 2 * n + i : 2 * n + i + 1, :] = share[:, 128 * i : 128 * (i + 1)]
 
     def backward(first, last):
         @pl.loop(first, last)
@@ -325,18 +336,13 @@
             for n in range(B // 256):
                 c = pl.ds(n * 256, 256)
                 g = unpacked(gb[b])[:, n * 256 : (n + 1) * 256]
-                dn = lax.dot_general(
-                    cot[...], wb[b, c, :], (((1,), (1,)), ((), ())), preferred_element_type=F32
-                )
                 xf = xb[b, :, c].astype(F32)
-                rs = rstd[:, 0:1]
-                xb[b, :, c] = (rs * (dn * g - xf * slope[:, 0:1])).astype(BF16)
-                share = jnp.sum(dn * xf * rs, axis=0, keepdims=True)
-                for i in range(2):
-                    ggs[b, 2 * n + i : 2 * n + i + 1, :] = share[:, 128 * i : 128 * (i + 1)]
+                xb[b, :, c] = (rstd[:, 0:1] * (product(b, n) * g - xf * slope[:, 0:1])).astype(BF16)
 
     ggs[...] = jnp.zeros_like(ggs)
-    backward(0, 4)
+    gain_shares(0, 6)
+    gain_shares(7, 8)
+    gg = [send(ggs.at[i], ggr.at[back(i)], peer(i // 4, i % 4)) for i in (1, 2, 3, 4, 5, 7)]
 
     exponents = [exp_ref[i] for i in range(ROUNDS)]
     m_in.wait()
@@ -390,8 +396,6 @@
 
     own_gradient(0)
     step(0)
-    backward(4, 8)
-    gg = [send(ggs.at[i], ggr.at[back(i)], peer(i // 4, i % 4)) for i in range(1, 8)]
     partial_right(1)
     step(1)
     partial_left(1)
@@ -401,6 +405,19 @@
     own_gradient(1)
     mix(1)
     settle(early)
+    step(2)
+    step(3)
+    for copy in (a4r, a4l, a4z):
+        copy.wait_recv()
+    add_values(6)
+    gain_shares(6, 7)
+    gg.append(send(ggs.at[6], ggr.at[back(6)], peer(1, 2)))
+    step(4)
+    slopes()
+    step(5)
+
+    mix(2)
+    mix(3)
 
     for copy in gg:
         copy.wait_recv()
@@ -413,21 +430,16 @@
     gxs[...] = packed(stepped.astype(F32))
     gx = [send(gxs, gxr.at[j], mate(j)) for j in range(1, 8)]
 
-    step(2)
-    finish(0)
-    step(3)
+    backward(0, 2)
+    mix(4)
+    mix(5)
+    for p in range(2):
+        finish(p)
+    backward(2, 8)
     for copy in gx:
         copy.wait_recv()
     parts = averaged([gxs[...]] + [gxr[j] for j in range(1, 8)], exponents)
     gout[0:1, :] = unpacked(parts[0])
-    finish(1)
-    step(4)
-    step(5)
-    mix(2)
-    mix(3)
-    settle(ready)
-    mix(4)
-    mix(5)
     settle(len(sent) - 28)
     for p in range(2, len(PIECES)):
         finish(p)

time: 132 us -> 130 us (0.985)
  Pallas kernels: 131 us -> 129 us
    pallas_call x1, Pallas kernels: 127 us -> 125 us  [local(): pl.pallas_call(kernel, out_shape=[pltpu.VMEM(s, t) for s, t in held], in_...]
where the time goes in v4:
time: 130 us
  Pallas kernels  129 us (99%)
    pallas_call x1, Pallas kernels, local(): pl.pallas_call(kernel, out_shape=[pltpu.VMEM(s, t) for s, t in held], in_...  125 us
    pallas_call x1, Pallas kernels, local(): pl.pallas_call(write_out, out_shape=[jax.ShapeDtypeStruct(s, t) for s, t...  4.6 us

profile of v4, /device:TPU:1, one launch (start us, length us, event | category | flops | bytes accessed | tf_op | source)
XLA Modules:
  0.0 129.9 jit_solution(10207611303120439090)
XLA Ops:
  0.6 124.6 %layer_step.1 = (bf16[512,1024]{1,0:T(8,128)(2,1)S(1)}, bf16[8,512,512]{2,1,0:T(8,128)(2,1)S(1)}, bf16[512,1024]{1,0:T(8,128)(2,1)S(1)}, f32[512,1024]{1,0:T(8,1...) custom-call(bf16[1,512,4096]{2,1,0:T(8,128)(2,1)} %x_hbm.1, bf16[1,512]{1,0:T(2,128)(2,1)} %gain_ref.1, ...), custom_call_target="tpu_custom_call" | custom-call | flops 12884901888 | bytes 20971520 | tf_op jit(solution)/shard_map/layer_step/pallas_call | solution.py:486
  125.3 4.6 %write_out.1 = (bf16[1,512,1024]{2,1,0:T(8,128)(2,1)}, bf16[1,512,4096]{2,1,0:T(8,128)(2,1)}, bf16[1,512,1024]{2,1,0:T(8,128)(2,1)}, f32[1,512,1024]{2,1,0:T(8,1...) custom-call(bf16[512,1024]{1,0:T(8,128)(2,1)S(1)} %get-tuple-element.14.vout, ...), custom_call_target="tpu_custom_call" | custom-call | tf_op jit(solution)/shard_map/write_out/pallas_call | solution.py:499

commit v5 on v4

--- a/solution.py
+++ b/solution.py
@@ -413,8 +413,8 @@
     gain_shares(6, 7)
     gg.append(send(ggs.at[6], ggr.at[back(6)], peer(1, 2)))
     step(4)
+    step(5)
     slopes()
-    step(5)
 
     mix(2)
     mix(3)

time: 130 us -> 130 us (level)
  no operation moved by 1% of the time
where the time goes in v5:
time: 130 us
  Pallas kernels  129 us (99%)
    pallas_call x1, Pallas kernels, local(): pl.pallas_call(kernel, out_shape=[pltpu.VMEM(s, t) for s, t in held], in_...  125 us
    pallas_call x1, Pallas kernels, local(): pl.pallas_call(write_out, out_shape=[jax.ShapeDtypeStruct(s, t) for s, t...  4.6 us

profile of v5, /device:TPU:1, one launch (start us, length us, event | category | flops | bytes accessed | tf_op | source)
XLA Modules:
  0.0 129.9 jit_solution(9584804961118179006)
XLA Ops:
  0.6 124.6 %layer_step.1 = (bf16[512,1024]{1,0:T(8,128)(2,1)S(1)}, bf16[8,512,512]{2,1,0:T(8,128)(2,1)S(1)}, bf16[512,1024]{1,0:T(8,128)(2,1)S(1)}, f32[512,1024]{1,0:T(8,1...) custom-call(bf16[1,512,4096]{2,1,0:T(8,128)(2,1)} %x_hbm.1, bf16[1,512]{1,0:T(2,128)(2,1)} %gain_ref.1, ...), custom_call_target="tpu_custom_call" | custom-call | flops 12884901888 | bytes 20971520 | tf_op jit(solution)/shard_map/layer_step/pallas_call | solution.py:486
  125.3 4.6 %write_out.1 = (bf16[1,512,1024]{2,1,0:T(8,128)(2,1)}, bf16[1,512,4096]{2,1,0:T(8,128)(2,1)}, bf16[1,512,1024]{2,1,0:T(8,128)(2,1)}, f32[1,512,1024]{2,1,0:T(8,1...) custom-call(bf16[512,1024]{1,0:T(8,128)(2,1)S(1)} %get-tuple-element.14.vout, ...), custom_call_target="tpu_custom_call" | custom-call | tf_op jit(solution)/shard_map/write_out/pallas_call | solution.py:499
